TPU v7x, 512 devices: a whole 4x4x16 slice. The times are simulated.
512 devices in a mesh: dp: 8 (over y, core), ctx: 64 (over z, x).
Axes of the slice: x: 4, y: 4, z: 16, core: 2. Of those that a mesh axis runs over, the one named last changes fastest.
Arguments:
- features_in: bfloat16 [1536, 65536], P(None, ('dp', 'ctx')), parts along dimension 1, may hold values from -6 to 6
- short_weight: float32 [1536, 3], replicated, may hold values from -3.5 to 3.5
- long_filter: float32 [512, 8192], P(None, 'ctx'), may hold values from -3.5 to 3.5
- skip_gain: float32 [512], replicated, may hold values from -1 to 1
Outputs:
- mixed_out: float32 [512, 65536], P(None, ('dp', 'ctx')), parts along dimension 1
There are 8 independent parts, one for each index of `dp`. A program takes and returns all parts, laid end to end along the dimension named above; an argument that names none is the same for every part. Nothing has to cross between parts.
All inputs are finite; a program needn't handle non-finite values.
Results may differ from a plain program's by a relative error of at most 0.0003.
Values may be sent and summed in bfloat16 or wider, within the bound.
A program may use at most 64 MiB of HBM per device.

v0:
```python
import math

import jax
import jax.numpy as jnp
from jax import lax
from jax.sharding import PartitionSpec as P

precise = lax.Precision.HIGHEST


def from_behind(value, axis, steps):
    count = lax.axis_size(axis)
    first, last = (max(0, -steps), min(count, count - steps))
    return lax.ppermute(value, axis, [(source, source + steps) for source in range(first, last)])


def complex_apply(values, table_re, table_im):
    part_re = values[0]
    part_im = values[1]
    out_re = jnp.einsum("...t,tk->...k", part_re, table_re, precision=precise) - jnp.einsum(
        "...t,tk->...k", part_im, table_im, precision=precise
    )
    out_im = jnp.einsum("...t,tk->...k", part_re, table_im, precision=precise) + jnp.einsum(
        "...t,tk->...k", part_im, table_re, precision=precise
    )
    return jnp.stack([out_re, out_im])


def complex_across(values, table_re, table_im):
    part_re = values[0]
    part_im = values[1]
    out_re = jnp.einsum("...ab,ak->...kb", part_re, table_re, precision=precise) - jnp.einsum(
        "...ab,ak->...kb", part_im, table_im, precision=precise
    )
    out_im = jnp.einsum("...ab,ak->...kb", part_re, table_im, precision=precise) + jnp.einsum(
        "...ab,ak->...kb", part_im, table_re, precision=precise
    )
    return jnp.stack([out_re, out_im])


def complex_times(left, right):
    return jnp.stack(
        [left[0] * right[0] - left[1] * right[1], left[0] * right[1] + left[1] * right[0]]
    )


def phase_table(phases, modulus):
    angles = phases.astype(jnp.float32) * (-2.0 * math.pi / modulus)
    return (jnp.cos(angles), jnp.sin(angles))


def spectrum_table(block_rows):
    inner = jnp.arange(block_rows, dtype=jnp.int32)
    phases = inner[:, None] * inner[None, :] % block_rows
    return phase_table(phases, block_rows)


def channel_convolve(gated_rows, filter_rows, devices, block_rows):
    seq_total = devices * block_rows
    channel_rows = gated_rows.shape[0]
    whole_angle = jnp.arange(seq_total, dtype=jnp.float32) * (math.pi / seq_total)
    whole_cos = jnp.cos(whole_angle)[None, :]
    whole_sin = jnp.sin(whole_angle)[None, :]

    def paired_whole(signal):
        empty_part = jnp.zeros_like(signal)
        stacked = jnp.stack(
            [jnp.stack([signal, signal * whole_cos]), jnp.stack([empty_part, -signal * whole_sin])]
        )
        return stacked.reshape(2, 2, channel_rows, devices, block_rows)

    outer_index = jnp.arange(devices, dtype=jnp.int32)
    inner_index = jnp.arange(block_rows, dtype=jnp.int32)
    outer_re, outer_im = phase_table(outer_index[:, None] * outer_index[None, :] % devices, devices)
    turn_re, turn_im = phase_table(
        outer_index[:, None] * inner_index[None, :] % seq_total, seq_total
    )
    turn_fwd = jnp.stack([turn_re, turn_im])
    turn_back = jnp.stack([turn_re, -turn_im])
    local_re, local_im = spectrum_table(block_rows)

    def forward(values):
        values = complex_across(values, outer_re, outer_im)
        values = complex_times(values, turn_fwd)
        return complex_apply(values, local_re, local_im)

    product = complex_times(forward(paired_whole(gated_rows)), forward(paired_whole(filter_rows)))
    result = complex_apply(product, local_re.T, -local_im.T) / block_rows
    result = complex_times(result, turn_back)
    result = complex_across(result, outer_re.T, -outer_im.T) / devices
    result = result.reshape(2, 2, channel_rows, seq_total)
    return 0.5 * (result[0, 0] + result[0, 1] * whole_cos - result[1, 1] * whole_sin)


def body(features_in, short_weight, long_filter, skip_gain):
    channel_count = long_filter.shape[0]
    block_rows = features_in.shape[1]
    tap_count = short_weight.shape[1]
    previous = from_behind(features_in[:, block_rows - (tap_count - 1) :], "ctx", 1)
    extended = jnp.concatenate([previous, features_in], axis=1).astype(jnp.float32)
    featurized = jnp.zeros((3 * channel_count, block_rows), jnp.float32)
    for offset in range(tap_count):
        start = tap_count - 1 - offset
        featurized = (
            featurized + short_weight[:, offset][:, None] * extended[:, start : start + block_rows]
        )
    query_part = featurized[:channel_count]
    key_part = featurized[channel_count : 2 * channel_count]
    value_part = featurized[2 * channel_count :]
    gated_input = key_part * value_part
    devices = lax.axis_size("ctx")
    gated_rows, filter_rows = (
        lax.all_to_all(gated_input, "ctx", split_axis=0, concat_axis=1, tiled=True),
        lax.all_to_all(long_filter, "ctx", split_axis=0, concat_axis=1, tiled=True),
    )
    convolved_rows = channel_convolve(gated_rows, filter_rows, devices, block_rows)
    convolved = lax.all_to_all(convolved_rows, "ctx", split_axis=1, concat_axis=0, tiled=True)
    convolved = convolved + skip_gain[:, None] * gated_input
    return query_part * convolved


def solution(mesh):
    in_specs = (P(None, ("dp", "ctx")), P(), P(None, "ctx"), P())
    out_specs = P(None, ("dp", "ctx"))
    return jax.shard_map(body, mesh=mesh, in_specs=in_specs, out_specs=out_specs, check_vma=False)
```

profile of v0, /device:TPU:24, one launch (start us, length us, event | category | flops | bytes accessed | tf_op | source)
XLA Modules:
  0.0 128.4 jit_solution(1685865645863065932)
XLA Ops:
  0.0 18.7 %all-to-all-start.1 = ((f32[64,8,128]{2,1,0:T(8,128)}), f32[64,8,128]{2,1,0:T(8,128)S(1)}, u32[]{:S(2)}, u32[]{:S(2)}) async-start(f32[64,8,128]{2,1,0:T(8,128)} %bitcast.209), calls=%async_computation.1 | async-start | bytes 524288 | tf_op jit(solution)/shard_map/all_to_all | solution.py:114
  18.7 1.2 slice.56
  19.9 3.5 %collective-permute-start = (bf16[1536,2]{1,0:T(8,128)(2,1)S(1)}, bf16[1536,2]{1,0:T(8,128)(2,1)S(1)}, u32[]{:S(2)}, u32[]{:S(2)}) collective-permute-start(bf16[1536,2]{1,0:T(8,128)(2,1)S(1)} %slice.56), channel_id=1, source_target_pairs={{0,1},{1,2},{2,3},{3,4},{4,5},{5,6},{6,7},{7,8},{8,9},{9,10},{10,1... | collective-permute-start | bytes 18440 | tf_op jit(solution)/shard_map/ppermute | solution.py:14
  23.4 0.9 slice_reduce_fusion.2
  24.3 9.1 %collective-permute-done = bf16[1536,2]{1,0:T(8,128)(2,1)S(1)} collective-permute-done((bf16[1536,2]{1,0:T(8,128)(2,1)S(1)}, bf16[1536,2]{1,0:T(8,128)(2,1)S(1)}, u32[]{:S(2)}, u32[]{:S(2)}) %collective-permute-start) | collective-permute-done | bytes 6176 | tf_op jit(solution)/shard_map/ppermute | solution.py:14
  33.7 1.2 fusion.4
  35.7 5.5 %all-to-all-done.1 = f32[64,8,128]{2,1,0:T(8,128)S(1)} async-done(((f32[64,8,128]{2,1,0:T(8,128)}), f32[64,8,128]{2,1,0:T(8,128)S(1)}, u32[]{:S(2)}, u32[]{:S(2)}) %all-to-all-start.1) | async-done | bytes 262176 | tf_op jit(solution)/shard_map/all_to_all | solution.py:114
  41.2 15.0 %all-to-all-start = ((f32[64,8,128]{2,1,0:T(8,128)}), f32[64,8,128]{2,1,0:T(8,128)S(1)}, u32[]{:S(2)}, u32[]{:S(2)}) async-start(f32[64,8,128]{2,1,0:T(8,128)} %fusion.35), calls=%async_computation | async-start | bytes 524288 | tf_op jit(solution)/shard_map/all_to_all | solution.py:113
  58.1 20.2 %all-to-all-done = f32[64,8,128]{2,1,0:T(8,128)S(1)} async-done(((f32[64,8,128]{2,1,0:T(8,128)}), f32[64,8,128]{2,1,0:T(8,128)S(1)}, u32[]{:S(2)}, u32[]{:S(2)}) %all-to-all-start) | async-done | bytes 262176 | tf_op jit(solution)/shard_map/all_to_all | solution.py:113
  78.4 0.8 bitcast_negate_fusion
  80.0 0.8 fusion.27
  80.9 0.8 broadcast_multiply_fusion
  81.7 0.8 convolution_add_fusion.4
  82.5 0.8 convolution_subtract_fusion.3
  83.3 0.8 fusion.12
  84.1 0.8 fusion.14
  85.0 0.8 fusion.28
  86.5 0.8 convolution_add_fusion.5
  87.3 0.8 convolution_subtract_fusion.5
  88.1 0.8 fusion.18
  88.9 0.8 fusion.20
  89.8 0.8 convolution_add_fusion.2
  90.6 0.8 convolution_subtract_fusion.2
  91.4 1.0 convolution_subtract_fusion.4
  92.5 0.9 multiply_add_fusion.1
  93.3 0.8 fusion.41
  94.2 0.8 fusion.49
  95.0 0.8 fusion.3
  95.8 0.8 fusion.2
  99.1 0.8 fusion.1
  101.0 26.5 %all_to_all.48 = f32[8,64,128]{2,0,1:T(8,128)S(1)} all-to-all(f32[8,64,128]{2,0,1:T(8,128)S(1)} %copy.40), channel_id=1, replica_groups=mesh['dp'=8,'ctx'=64] {'ctx'}, dimensions={1} | all-to-all | bytes 524288 | tf_op jit(solution)/shard_map/all_to_all | solution.py:117
  127.6 0.9 slice_multiply_fusion.4
  (33 shorter events, 8.3 us)
Async XLA Ops:
  0.0 33.4 %copy-start = (bf16[1536,128]{1,0:T(8,128)(2,1)S(1)}, bf16[1536,128]{1,0:T(8,128)(2,1)}, u32[]{:S(2)}) copy-start(bf16[1536,128]{1,0:T(8,128)(2,1)} %param.4) | copy-start | bytes 1179652
  0.0 41.2 %all-to-all-start.1 = ((f32[64,8,128]{2,1,0:T(8,128)}), f32[64,8,128]{2,1,0:T(8,128)S(1)}, u32[]{:S(2)}, u32[]{:S(2)}) async-start(f32[64,8,128]{2,1,0:T(8,128)} %bitcast.209), calls=%async_computation.1 | async-start | bytes 524288 | tf_op jit(solution)/shard_map/all_to_all | solution.py:114
  19.9 13.5 %collective-permute-start = (bf16[1536,2]{1,0:T(8,128)(2,1)S(1)}, bf16[1536,2]{1,0:T(8,128)(2,1)S(1)}, u32[]{:S(2)}, u32[]{:S(2)}) collective-permute-start(bf16[1536,2]{1,0:T(8,128)(2,1)S(1)} %slice.56), channel_id=1, source_target_pairs={{0,1},{1,2},{2,3},{3,4},{4,5},{5,6},{6,7},{7,8},{8,9},{9,10},{10,1... | collective-permute-start | bytes 18440 | tf_op jit(solution)/shard_map/ppermute | solution.py:14
  41.2 37.2 %all-to-all-start = ((f32[64,8,128]{2,1,0:T(8,128)}), f32[64,8,128]{2,1,0:T(8,128)S(1)}, u32[]{:S(2)}, u32[]{:S(2)}) async-start(f32[64,8,128]{2,1,0:T(8,128)} %fusion.35), calls=%async_computation | async-start | bytes 524288 | tf_op jit(solution)/shard_map/all_to_all | solution.py:113
  79.2 1.5 %copy-start.1 = (f32[8,64,128]{2,1,0:T(8,128)S(1)}, f32[8,64,128]{2,1,0:T(8,128)}, u32[]{:S(2)}) copy-start(f32[8,64,128]{2,1,0:T(8,128)} %get-tuple-element.13) | copy-start | bytes 786436
  100.0 0.8 copy-start.2
  100.1 27.5 %copy-start.3 = (f32[512]{0:T(512)S(1)}, f32[512]{0:T(512)}, u32[]{:S(2)}) copy-start(f32[512]{0:T(512)} %param.7) | copy-start | bytes 6148
where the time goes:
time: 129 us; the launch traced here: 128 us
  starting transfers between devices  37.2 us (29%)
  waiting for transfers between devices  34.8 us (27%)
  blocking collectives  26.5 us (21%)
  matrix products  19.2 us (15%)
  other arithmetic  6.96 us (5%)
  local copies, waits for them, and re-layouts  3.37 us (3%)
    all_to_all x1, blocking collectives, body(): lax.all_to_all(convolved_rows, 'ctx', split_axis=1, concat_axis=0, tiled=...  26.5 us
    all_to_all x1, waiting for transfers between devices, body(): lax.all_to_all(gated_input, 'ctx', split_axis=0, concat_axis=1, tiled=True)  20.2 us
    all_to_all x1, starting transfers between devices, body(): lax.all_to_all(long_filter, 'ctx', split_axis=0, concat_axis=1, tiled=True)  18.7 us
    all_to_all x1, starting transfers between devices, body(): lax.all_to_all(gated_input, 'ctx', split_axis=0, concat_axis=1, tiled=True)  15 us
    ppermute x1, waiting for transfers between devices, from_behind(): lax.ppermute(value, axis, [(source, source + steps) for source in range(f...  9.13 us
    all_to_all x1, waiting for transfers between devices, body(): lax.all_to_all(long_filter, 'ctx', split_axis=0, concat_axis=1, tiled=True)  5.46 us
    ppermute x1, starting transfers between devices, from_behind(): lax.ppermute(value, axis, [(source, source + steps) for source in range(f...  3.5 us
    dot_general x3, matrix products, complex_apply(): jnp.einsum('...t,tk->...k', part_im, table_im, precision=precise)  2.69 us
  transfers between devices with their start and end apart: 3, of which 3 were waited for; matrix products, arithmetic and copies ran while one was open for 5% of the time, Pallas kernels for 0%

commit v1 on v0

v1 whole, which is shorter than its diff:
```python
import functools
import math

import jax
import jax.numpy as jnp
import numpy as np
from jax import lax
from jax.experimental import pallas as pl
from jax.experimental.pallas import tpu as pltpu
from jax.sharding import PartitionSpec as P

MESH = pl.DeviceIdType.MESH
F32, BF16 = jnp.float32, jnp.bfloat16
RINGS = (16, 4)
CTX = RINGS[0] * RINGS[1]
LANES = 128
OWN = 8
LIFT = 2.0**7.5
SLOT = 16


def coded(value, largest):
    ratio = jnp.where(largest > 1e-30, LIFT / jnp.maximum(largest, 1e-30), 0.0)
    power = value * ratio
    for _ in range(4):
        power = power * power
    return jnp.where(value < 0, -power, power)


def decoded(code):
    size = jnp.abs(code)
    root = jnp.exp(jnp.log(jnp.maximum(size, 1e-37)) * (1.0 / 16.0)) * (1.0 / LIFT)
    root = jnp.where(size > 1e-37, root, 0.0)
    return jnp.where(code < 0, -root, root)


def farthest_first(index, extent):
    half, step = extent // 2, (index + 1) // 2
    return half + step * (1 - 2 * (index % 2))


def each_peer(visit):
    me = lax.axis_index("ctx")
    at_z, at_x = me // RINGS[1], me % RINGS[1]

    def one(index, carry):
        to_z = (at_z + farthest_first(index // RINGS[1], RINGS[0])) % RINGS[0]
        to_x = (at_x + farthest_first(index % RINGS[1], RINGS[1])) % RINGS[1]
        visit(to_z * RINGS[1] + to_x)
        return carry

    lax.fori_loop(0, CTX - 1, one, 0)


def send_blocks(*exchanges):
    me = lax.axis_index("ctx")

    def visit(peer):
        for source, target, sent, landed in exchanges:
            pltpu.make_async_remote_copy(
                src_ref=source.at[peer],
                dst_ref=target.at[me],
                send_sem=sent,
                recv_sem=landed,
                device_id={"ctx": peer},
                device_id_type=MESH,
            ).start()

    each_peer(visit)
    for source, target, _, landed in exchanges:
        pltpu.make_async_copy(source.at[me], target.at[me], landed).start()


def wait_landed(target, landed):
    pltpu.make_async_copy(target, target, landed).wait()


def wait_sent(source, sent):
    part = source.at[pl.ds(0, CTX - 1)]
    pltpu.make_async_copy(part, part, sent).wait()


def split(value):
    high = value.astype(BF16)
    return high, (value - high.astype(F32)).astype(BF16)


def spectrum(blocks, across, inner, turn_re, turn_im):
    high, low = split(jnp.concatenate(blocks, axis=1))
    outer = jnp.dot(across, jnp.concatenate([high, low, high, low], axis=0), preferred_element_type=F32)
    rows = []
    for c in range(OWN):
        part = outer[:, c * LANES : (c + 1) * LANES]
        re, im = part[:CTX], part[CTX:]
        rows.append(jnp.concatenate([re * turn_re - im * turn_im, re * turn_im + im * turn_re], axis=1))
    high, low = split(jnp.concatenate(rows, axis=0))
    return jnp.dot(jnp.concatenate([high, low, high], axis=1), inner, preferred_element_type=F32)


def inverse(product, across, inner, turn_re, turn_im):
    high, low = split(product)
    mixed = jnp.dot(jnp.concatenate([high, low, high], axis=1), inner, preferred_element_type=F32)
    columns = []
    for c in range(OWN):
        part = mixed[c * CTX : (c + 1) * CTX]
        re, im = part[:, :LANES], part[:, LANES:]
        columns.append(jnp.concatenate([re * turn_re + im * turn_im, im * turn_re - re * turn_im], axis=0))
    high, low = split(jnp.concatenate(columns, axis=1))
    return jnp.dot(across, jnp.concatenate([high, low, high], axis=0), preferred_element_type=F32)


def lane_of(shape):
    return lax.broadcasted_iota(jnp.int32, shape, len(shape) - 1)


def kernel(
    feat_hbm, short_hbm, filt_hbm, skip_hbm, fwd_across_hbm, fwd_inner_hbm, inv_inner_hbm, inv_across_hbm, turn_hbm,
    out_ref,
    feat, short, filt, skip, fwd_across, fwd_inner, inv_inner, inv_across, turn,
    edge_rows, edge_wide, plane, plane_h,
    gate_src, edge_src, filt_src, gate_dst, edge_dst, filt_dst,
    conv_src, peak_src, conv_dst, peak_dst, query_tail,
    load_sem, sent, landed,
):
    me = lax.axis_index("ctx")
    barrier = pltpu.get_barrier_semaphore()
    each_peer(lambda peer: pl.semaphore_signal(barrier, inc=1, device_id={"ctx": peer}, device_id_type=MESH))

    pairs = (
        (feat_hbm, feat), (short_hbm, short), (filt_hbm, filt), (skip_hbm, skip), (fwd_across_hbm, fwd_across),
        (fwd_inner_hbm, fwd_inner), (inv_inner_hbm, inv_inner), (inv_across_hbm, inv_across), (turn_hbm, turn),
    )
    loads = [pltpu.make_async_copy(source, target, load_sem.at[i]) for i, (source, target) in enumerate(pairs)]
    for load in loads:
        load.start()
    for load in loads:
        load.wait()

    count = OWN * CTX
    chunk = 8 * OWN
    lane = lane_of((chunk, LANES))

    def local_feature(row):
        rows = pl.ds(row, chunk)
        value = feat[rows, :].astype(F32)
        taps = short[rows, :]
        once, twice = pltpu.roll(value, 1, axis=1), pltpu.roll(value, 2, axis=1)
        near = taps[:, 1:2] * once
        far = taps[:, 2:3] * twice
        zero = jnp.zeros_like(value)
        inside = taps[:, 0:1] * value + jnp.where(lane >= 1, near, zero) + jnp.where(lane >= 2, far, zero)
        beyond = jnp.where(lane < 1, near, zero) + jnp.where(lane < 2, far, zero)
        return inside, beyond

    for i in range(count // chunk):
        row = i * chunk
        zero = jnp.zeros((chunk, LANES), F32)
        key, key_beyond = local_feature(count + row)
        value, value_beyond = local_feature(2 * count + row)
        gated = key * value
        gated = jnp.where(lane >= 2, gated, zero)
        taps = filt[pl.ds(row, chunk), :]
        gated_peak = jnp.max(jnp.abs(gated), axis=1, keepdims=True)
        taps_peak = jnp.max(jnp.abs(taps), axis=1, keepdims=True)
        edge = (
            jnp.where(lane < 2, key, zero)
            + pltpu.roll(jnp.where(lane < 2, value, zero), 2, axis=1)
            + pltpu.roll(key_beyond, 4, axis=1)
            + pltpu.roll(value_beyond, 6, axis=1)
        )
        edge = jnp.where(lane == 8, gated_peak, jnp.where(lane == 9, taps_peak, edge))
        edge_rows[pl.ds(row, chunk), :] = edge
        owners = pl.ds(i * 8, 8)
        gate_src[owners] = coded(gated, gated_peak).reshape(8, OWN, LANES).astype(BF16)
        filt_src[owners] = coded(taps, taps_peak).reshape(8, OWN, LANES).astype(BF16)

    wide = edge_rows[pl.ds(0, CTX, stride=OWN), :]
    for c in range(1, OWN):
        wide = wide + pltpu.roll(edge_rows[pl.ds(c, CTX, stride=OWN), :], SLOT * c, axis=1)
    edge_wide[...] = wide
    for q in range(CTX):
        edge_src[q] = edge_wide[q : q + 1, :]

    pl.semaphore_wait(barrier, CTX - 1)
    send_blocks((gate_src, gate_dst, sent.at[0], landed.at[0]), (edge_src, edge_dst, sent.at[1], landed.at[1]))
    send_blocks((filt_src, filt_dst, sent.at[2], landed.at[2]))
    tail_copy = pltpu.make_async_remote_copy(
        src_ref=feat.at[pl.ds(0, count)],
        dst_ref=query_tail,
        send_sem=sent.at[5],
        recv_sem=landed.at[5],
        device_id={"ctx": (me + 1) % CTX},
        device_id_type=MESH,
    )
    tail_copy.start()

    turn_re, turn_im = turn[:CTX], turn[CTX:]
    wait_landed(gate_dst, landed.at[0])
    wait_landed(edge_dst, landed.at[1])
    for p in range(CTX):
        edge_wide[p : p + 1, :] = edge_dst[p]
    for i in range(8):
        part = decoded(gate_dst[pl.ds(i * 8, 8)].astype(F32))
        plane[pl.ds(i * chunk, chunk), :] = part.reshape(chunk, LANES)
    edge = edge_wide[...]
    row_of = lax.broadcasted_iota(jnp.int32, (CTX, LANES), 0)
    before = jnp.where(row_of >= 1, pltpu.roll(edge, 1, axis=0), 0.0)
    whole = edge + pltpu.roll(before, LANES - 4, axis=1)
    first = whole * pltpu.roll(whole, LANES - 2, axis=1)
    lane = lane_of((CTX, LANES))
    blocks = []
    for c in range(OWN):
        at = SLOT * c
        block = plane[pl.ds(c, CTX, stride=OWN), :] * edge[:, at + 8 : at + 9]
        block = jnp.where(lane == 0, first[:, at : at + 1], block)
        blocks.append(jnp.where(lane == 1, first[:, at + 1 : at + 2], block))
    seen = spectrum(blocks, fwd_across[...], fwd_inner[...], turn_re, turn_im)

    wait_landed(filt_dst, landed.at[2])
    for i in range(8):
        part = decoded(filt_dst[pl.ds(i * 8, 8)].astype(F32))
        plane_h[pl.ds(i * chunk, chunk), :] = part.reshape(chunk, LANES)
    taps = [plane_h[pl.ds(c, CTX, stride=OWN), :] * edge[:, SLOT * c + 9 : SLOT * c + 10] for c in range(OWN)]
    response = spectrum(taps, fwd_across[...], fwd_inner[...], turn_re, turn_im)
    s_re, s_im = seen[:, :LANES], seen[:, LANES:]
    r_re, r_im = response[:, :LANES], response[:, LANES:]
    product = jnp.concatenate([s_re * r_re - s_im * r_im, s_re * r_im + s_im * r_re], axis=1)
    result = inverse(product, inv_across[...], inv_inner[...], turn_re, turn_im)

    peaks = jnp.zeros((CTX, LANES), F32)
    for c in range(OWN):
        part = result[:, c * LANES : (c + 1) * LANES] + skip[me * OWN + c] * blocks[c]
        peak = jnp.max(jnp.abs(part), axis=1, keepdims=True)
        peaks = jnp.where(lane == c, peak, peaks)
        plane[pl.ds(c, CTX, stride=OWN), :] = coded(part, peak)
    edge_wide[...] = peaks
    for q in range(CTX):
        peak_src[q] = edge_wide[q : q + 1, :]
    for i in range(8):
        conv_src[pl.ds(i * 8, 8)] = plane[pl.ds(i * chunk, chunk), :].reshape(8, OWN, LANES).astype(BF16)

    send_blocks((conv_src, conv_dst, sent.at[3], landed.at[3]), (peak_src, peak_dst, sent.at[4], landed.at[4]))

    tail_copy.wait_recv()
    lane = lane_of((chunk, LANES))
    keep = jnp.where(me > 0, 1.0, 0.0)
    for i in range(count // chunk):
        rows = pl.ds(i * chunk, chunk)
        value, tail = feat[rows, :].astype(F32), query_tail[rows, :].astype(F32) * keep
        taps = short[rows, :]
        query = taps[:, 0:1] * value
        for step in (1, 2):
            moved = jnp.where(lane < step, pltpu.roll(tail, step, axis=1), pltpu.roll(value, step, axis=1))
            query = query + taps[:, step : step + 1] * moved
        plane_h[rows, :] = query

    wait_landed(conv_dst, landed.at[3])
    wait_landed(peak_dst, landed.at[4])
    shape = (8, OWN, LANES)
    mine = lane_of(shape) == lax.broadcasted_iota(jnp.int32, shape, 1)
    for i in range(8):
        rows = pl.ds(i * chunk, chunk)
        peak = jnp.broadcast_to(peak_dst[pl.ds(i * 8, 8)], shape)
        peak = jnp.sum(jnp.where(mine, peak, 0.0), axis=2, keepdims=True)
        part = decoded(conv_dst[pl.ds(i * 8, 8)].astype(F32)) * peak
        out_ref[rows, :] = plane_h[rows, :] * part.reshape(chunk, LANES)

    for slot, source in enumerate((gate_src, edge_src, filt_src, conv_src, peak_src)):
        wait_sent(source, sent.at[slot])
    tail_copy.wait_send()


def halves(table):
    high = table.astype(jnp.bfloat16)
    return high, (table - high.astype(np.float64)).astype(jnp.bfloat16)


def tables():
    points = 2 * CTX * LANES
    j, s, k1, k2 = np.arange(CTX), np.arange(LANES), np.arange(CTX) + 0.5, np.arange(LANES)
    outer = 2 * math.pi / LANES * np.outer(k1, j)
    high, low = halves(np.concatenate([np.cos(outer), -np.sin(outer)], axis=0))
    fwd_across = np.concatenate([high, high, low, low], axis=1)
    high, low = halves(np.concatenate([np.cos(outer.T), -np.sin(outer.T)], axis=1) * (2.0 / points))
    inv_across = np.concatenate([high, high, low], axis=1)
    inner = 2 * math.pi / LANES * (np.outer(s, k2) % LANES)
    cos, sin = np.cos(inner), np.sin(inner)
    high, low = halves(np.block([[cos, -sin], [sin, cos]]))
    fwd_inner = np.concatenate([high, high, low], axis=0)
    high, low = halves(np.block([[cos, sin], [-sin, cos]]))
    inv_inner = np.concatenate([high, high, low], axis=0)
    angle = 2 * math.pi / points * np.outer(k1, s)
    turn = np.concatenate([np.cos(angle), -np.sin(angle)], axis=0).astype(np.float32)
    return fwd_across, fwd_inner, inv_inner, inv_across, turn


def solution(mesh):
    constants = tables()

    def body(features_in, short_weight, long_filter, skip_gain):
        operands = (features_in, short_weight, long_filter, skip_gain, *map(jnp.asarray, constants))
        count = long_filter.shape[0]
        rows = (CTX, OWN, LANES)
        row = (CTX, 1, LANES)
        own_copies = [
            (pltpu.SMEM if value.ndim == 1 else pltpu.VMEM)(value.shape, value.dtype) for value in operands
        ]
        scratch = own_copies + [
            pltpu.VMEM((count, LANES), F32),
            pltpu.VMEM((CTX, LANES), F32),
            pltpu.VMEM((count, LANES), F32),
            pltpu.VMEM((count, LANES), F32),
            pltpu.VMEM(rows, BF16), pltpu.VMEM(row, F32), pltpu.VMEM(rows, BF16),
            pltpu.VMEM(rows, BF16), pltpu.VMEM(row, F32), pltpu.VMEM(rows, BF16),
            pltpu.VMEM(rows, BF16), pltpu.VMEM(row, F32),
            pltpu.VMEM(rows, BF16), pltpu.VMEM(row, F32),
            pltpu.VMEM((count, LANES), BF16),
            pltpu.SemaphoreType.DMA((len(operands),)),
            pltpu.SemaphoreType.DMA((6,)),
            pltpu.SemaphoreType.DMA((6,)),
        ]
        return pl.pallas_call(
            kernel,
            out_shape=jax.ShapeDtypeStruct((count, LANES), F32),
            in_specs=[pl.BlockSpec(memory_space=pl.ANY)] * len(operands),
            out_specs=pl.BlockSpec(memory_space=pltpu.VMEM),
            scratch_shapes=scratch,
            compiler_params=pltpu.CompilerParams(
                collective_id=0, has_side_effects=True, vmem_limit_bytes=48 * 1024 * 1024
            ),
        )(*operands)

    return jax.shard_map(
        body,
        mesh=mesh,
        in_specs=(P(None, ("dp", "ctx")), P(), P(None, "ctx"), P()),
        out_specs=P(None, ("dp", "ctx")),
        check_vma=False,
    )
```

time: 129 us -> 50.8 us (0.39)
  Pallas kernels: 0 us -> 44.2 us
  starting transfers between devices: 37.2 us -> 0 us
  waiting for transfers between devices: 34.8 us -> 0 us
  blocking collectives: 26.5 us -> 0 us
  matrix products: 19.2 us -> 0 us
  other arithmetic: 6.96 us -> 0 us
  local copies, waits for them, and re-layouts: 3.37 us -> 6.24 us
    pallas_call x0 -> x1, Pallas kernels: none -> 44.2 us  [body(): pl.pallas_call(kernel, out_shape=jax.ShapeDtypeStruct((count, LANES), F32...]
    all_to_all x2 -> x0, starting transfers between devices: 33.7 us -> none  [the longest x1 18.7 us: body(): lax.all_to_all(long_filter, 'ctx', split_axis=0, concat_axis=1, tiled=True)]
    all_to_all x1 -> x0, blocking collectives: 26.5 us -> none  [body(): lax.all_to_all(convolved_rows, 'ctx', split_axis=1, concat_axis=0, tiled=...]
    all_to_all x2 -> x0, waiting for transfers between devices: 25.7 us -> none  [the longest x1 20.2 us: body(): lax.all_to_all(gated_input, 'ctx', split_axis=0, concat_axis=1, tiled=True)]
    dot_general x24 -> x0, matrix products: 19.2 us -> none  [the longest x3 2.69 us: complex_apply(): jnp.einsum('...t,tk->...k', part_im, table_im, precision=precise)]
    ppermute x1 -> x0, waiting for transfers between devices: 9.13 us -> none  [from_behind(): lax.ppermute(value, axis, [(source, source + steps) for source in range(f...]
    unnamed x11 -> x18, local copies, waits for them, and re-layouts: 0.74 us -> 6.24 us
    ppermute x1 -> x0, starting transfers between devices: 3.5 us -> none  [from_behind(): lax.ppermute(value, axis, [(source, source + steps) for source in range(f...]
  transfers between devices with their start and end apart: 3 -> 0, of which waited for: 3 -> 0; matrix products, arithmetic and copies ran while one was open for 5% -> 0% of each run, Pallas kernels for 0% -> 0%
where the time goes in v1:
time: 50.8 us; the launch traced here: 50.5 us
  Pallas kernels  44.2 us (87%)
  local copies, waits for them, and re-layouts  6.24 us (12%)
    pallas_call x1, Pallas kernels, body(): pl.pallas_call(kernel, out_shape=jax.ShapeDtypeStruct((count, LANES), F32...  44.2 us
    unnamed x18, local copies, waits for them, and re-layouts  6.24 us

profile of v1, /device:TPU:24, one launch (start us, length us, event | category | flops | bytes accessed | tf_op | source)
XLA Modules:
  0.0 50.5 jit_solution(1492891064131638824)
XLA Ops:
  0.0 0.0 copy-start.1
  0.0 0.0 copy-start.7
  0.0 0.0 copy-start
  0.0 1.1 %copy.10.short_hbm = f32[1536,3]{1,0:T(8,128)S(1)} copy(f32[1536,3]{0,1:T(4,128)} %param.10) | data formatting | bytes 36864 | tf_op args[1]
  1.1 0.0 copy-done.1
  1.1 0.0 copy-done.7
  1.1 0.0 copy-done
  1.1 0.0 copy-start.2
  1.2 1.0 %copy-done.2 = bf16[768,256]{1,0:T(8,128)(2,1)S(1)} copy-done((bf16[768,256]{1,0:T(8,128)(2,1)S(1)}, bf16[768,256]{1,0:T(8,128)(2,1)}, u32[]{:S(2)}) %copy-start.2) | copy-done | bytes 393240
  2.1 0.0 copy-start.3
  2.1 0.9 %copy-done.3 = f32[512,128]{1,0:T(8,128)S(1)} copy-done((f32[512,128]{1,0:T(8,128)S(1)}, f32[512,128]{1,0:T(8,128)}, u32[]{:S(2)}) %copy-start.3) | copy-done | bytes 262168
  3.1 0.0 copy-start.4
  3.1 0.8 %copy-done.4 = f32[128,128]{1,0:T(8,128)S(1)} copy-done((f32[128,128]{1,0:T(8,128)S(1)}, f32[128,128]{1,0:T(8,128)}, u32[]{:S(2)}) %copy-start.4) | copy-done | bytes 65560
  3.9 0.0 copy-start.5
  3.9 0.8 %copy-done.5 = bf16[128,256]{1,0:T(8,128)(2,1)S(1)} copy-done((bf16[128,256]{1,0:T(8,128)(2,1)S(1)}, bf16[128,256]{1,0:T(8,128)(2,1)}, u32[]{:S(2)}) %copy-start.5) | copy-done | bytes 65560
  4.8 0.0 copy-start.6
  4.8 0.8 %copy-done.6 = bf16[64,384]{1,0:T(8,128)(2,1)S(1)} copy-done((bf16[64,384]{1,0:T(8,128)(2,1)S(1)}, bf16[64,384]{1,0:T(8,128)(2,1)}, u32[]{:S(2)}) %copy-start.6) | copy-done | bytes 49176
  5.6 44.2 %shard_map.91 = f32[512,128]{1,0:T(8,128)S(1)} custom-call(bf16[1536,128]{1,0:T(8,128)(2,1)S(1)} %copy-done, f32[1536,3]{1,0:T(8,128)S(1)} %copy.10.short_hbm, f32[512,128]{1,0:T(8,128)S(1)} %copy-done.3, f32[512]{0:T(512)S(1)} %copy-done.7, bf16[128,256]{1,0:T(8,128)(2,1)S(1)} %copy-done.5, bf16[768,256]{1,0:T(8,128)(2,1)S(1)} %copy-done.2, ...), custom_call_target="tpu_custom_call" | custom-call | tf_op jit(solution)/shard_map/pallas_call | solution.py:322
  49.8 0.7 %copy.12 = f32[512,128]{1,0:T(8,128)} copy(f32[512,128]{1,0:T(8,128)S(1)} %shard_map.91) | data formatting | bytes 524288
Async XLA Ops:
  0.0 1.1 %copy-start.1 = (bf16[768,256]{1,0:T(8,128)(2,1)S(1)}, bf16[768,256]{1,0:T(8,128)(2,1)}, u32[]{:S(2)}) copy-start(bf16[768,256]{1,0:T(8,128)(2,1)} %constant.12.clone.inv_inner_hbm) | copy-start | bytes 1179652
  0.0 1.1 %copy-start.7 = (f32[512]{0:T(512)S(1)}, f32[512]{0:T(512)}, u32[]{:S(2)}) copy-start(f32[512]{0:T(512)} %skip_hbm.1) | copy-start | bytes 6148
  0.0 1.1 %copy-start = (bf16[1536,128]{1,0:T(8,128)(2,1)S(1)}, bf16[1536,128]{1,0:T(8,128)(2,1)}, u32[]{:S(2)}) copy-start(bf16[1536,128]{1,0:T(8,128)(2,1)} %feat_hbm.1) | copy-start | bytes 1179652
  1.1 1.0 %copy-start.2 = (bf16[768,256]{1,0:T(8,128)(2,1)S(1)}, bf16[768,256]{1,0:T(8,128)(2,1)}, u32[]{:S(2)}) copy-start(bf16[768,256]{1,0:T(8,128)(2,1)} %constant.11.clone.fwd_inner_hbm) | copy-start | bytes 1179652
  2.1 0.9 %copy-start.3 = (f32[512,128]{1,0:T(8,128)S(1)}, f32[512,128]{1,0:T(8,128)}, u32[]{:S(2)}) copy-start(f32[512,128]{1,0:T(8,128)} %filt_hbm.1) | copy-start | bytes 786436
  3.1 0.8 %copy-start.4 = (f32[128,128]{1,0:T(8,128)S(1)}, f32[128,128]{1,0:T(8,128)}, u32[]{:S(2)}) copy-start(f32[128,128]{1,0:T(8,128)} %constant.14.clone.turn_hbm) | copy-start | bytes 196612
  3.9 0.8 %copy-start.5 = (bf16[128,256]{1,0:T(8,128)(2,1)S(1)}, bf16[128,256]{1,0:T(8,128)(2,1)}, u32[]{:S(2)}) copy-start(bf16[128,256]{1,0:T(8,128)(2,1)} %constant.10.clone.fwd_across_hbm) | copy-start | bytes 196612
  4.8 0.8 %copy-start.6 = (bf16[64,384]{1,0:T(8,128)(2,1)S(1)}, bf16[64,384]{1,0:T(8,128)(2,1)}, u32[]{:S(2)}) copy-start(bf16[64,384]{1,0:T(8,128)(2,1)} %constant.13.clone.inv_across_hbm) | copy-start | bytes 147460

commit v2 on v1

--- a/solution.py
+++ b/solution.py
@@ -116,8 +116,8 @@
 def kernel(
     feat_hbm, short_hbm, filt_hbm, skip_hbm, fwd_across_hbm, fwd_inner_hbm, inv_inner_hbm, inv_across_hbm, turn_hbm,
     out_ref,
-    feat, short, filt, skip, fwd_across, fwd_inner, inv_inner, inv_across, turn,
-    edge_rows, edge_wide, plane, plane_h,
+    feat, short_flat, filt, skip, fwd_across, fwd_inner, inv_inner, inv_across, turn,
+    short, edge_rows, edge_wide, plane, plane_h,
     gate_src, edge_src, filt_src, gate_dst, edge_dst, filt_dst,
     conv_src, peak_src, conv_dst, peak_dst, query_tail,
     load_sem, sent, landed,
@@ -127,7 +127,7 @@
     each_peer(lambda peer: pl.semaphore_signal(barrier, inc=1, device_id={"ctx": peer}, device_id_type=MESH))
 
     pairs = (
-        (feat_hbm, feat), (short_hbm, short), (filt_hbm, filt), (skip_hbm, skip), (fwd_across_hbm, fwd_across),
+        (feat_hbm, feat), (short_hbm, short_flat), (filt_hbm, filt), (skip_hbm, skip), (fwd_across_hbm, fwd_across),
         (fwd_inner_hbm, fwd_inner), (inv_inner_hbm, inv_inner), (inv_across_hbm, inv_across), (turn_hbm, turn),
     )
     loads = [pltpu.make_async_copy(source, target, load_sem.at[i]) for i, (source, target) in enumerate(pairs)]
@@ -139,6 +139,9 @@
     count = OWN * CTX
     chunk = 8 * OWN
     lane = lane_of((chunk, LANES))
+    for i in range(3 * count // LANES):
+        taps = jnp.concatenate([short_flat[:, i * LANES : (i + 1) * LANES], jnp.zeros((5, LANES), F32)], axis=0)
+        short[pl.ds(i * LANES, LANES), :] = taps.T
 
     def local_feature(row):
         rows = pl.ds(row, chunk)
@@ -298,7 +301,7 @@
     constants = tables()
 
     def body(features_in, short_weight, long_filter, skip_gain):
-        operands = (features_in, short_weight, long_filter, skip_gain, *map(jnp.asarray, constants))
+        operands = (features_in, short_weight.T, long_filter, skip_gain, *map(jnp.asarray, constants))
         count = long_filter.shape[0]
         rows = (CTX, OWN, LANES)
         row = (CTX, 1, LANES)
@@ -306,6 +309,7 @@
             (pltpu.SMEM if value.ndim == 1 else pltpu.VMEM)(value.shape, value.dtype) for value in operands
         ]
         scratch = own_copies + [
+            pltpu.VMEM((3 * count, 8), F32),
             pltpu.VMEM((count, LANES), F32),
             pltpu.VMEM((CTX, LANES), F32),
             pltpu.VMEM((count, LANES), F32),
@@ -322,11 +326,11 @@
         return pl.pallas_call(
             kernel,
             out_shape=jax.ShapeDtypeStruct((count, LANES), F32),
-            in_specs=[pl.BlockSpec(memory_space=pl.ANY)] * len(operands),
+            in_specs=[pl.BlockSpec(memory_space=pltpu.HBM)] * len(operands),
             out_specs=pl.BlockSpec(memory_space=pltpu.VMEM),
             scratch_shapes=scratch,
             compiler_params=pltpu.CompilerParams(
-                collective_id=0, has_side_effects=True, vmem_limit_bytes=48 * 1024 * 1024
+                collective_id=0, has_side_effects=True, vmem_limit_bytes=60 * 1024 * 1024
             ),
         )(*operands)
 

time: 50.8 us -> 46.9 us (0.923)
  local copies, waits for them, and re-layouts: 6.24 us -> 1.67 us
  Pallas kernels: 44.2 us -> 45.1 us
    unnamed x18 -> x1, local copies, waits for them, and re-layouts: 6.24 us -> 1.67 us
    pallas_call x1, Pallas kernels: 44.2 us -> 45.1 us  [body(): pl.pallas_call(kernel, out_shape=jax.ShapeDtypeStruct((count, LANES), F32...]
where the time goes in v2:
time: 46.9 us; the launch traced here: 46.7 us
  Pallas kernels  45.1 us (96%)
  local copies, waits for them, and re-layouts  1.67 us (4%)
    pallas_call x1, Pallas kernels, body(): pl.pallas_call(kernel, out_shape=jax.ShapeDtypeStruct((count, LANES), F32...  45.1 us
    unnamed x1, local copies, waits for them, and re-layouts  1.67 us

profile of v2, /device:TPU:24, one launch (start us, length us, event | category | flops | bytes accessed | tf_op | source)
XLA Modules:
  0.0 46.7 jit_solution(2757595637141915184)
XLA Ops:
  0.0 45.1 %shard_map.91 = f32[512,128]{1,0:T(8,128)} custom-call(bf16[1536,128]{1,0:T(8,128)(2,1)} %feat_hbm.1, f32[3,1536]{1,0:T(4,128)} %bitcast.1, f32[512,128]{1,0:T(8,128)} %filt_hbm.1, f32[512]{0:T(512)} %skip_hbm.1, bf16[128,256]{1,0:T(8,128)(2,1)} %constant.10.clone.fwd_across_hbm, bf16[768,256]{1,0:T(8,128)(2,1)} %constant.11.clone.fwd_inner_hbm, ...), custom_call_target="tpu_custom_call" | custom-call | tf_op jit(solution)/shard_map/pallas_call | solution.py:326
  45.1 1.7 %copy.11 = f32[512,128]{1,0:T(8,128)} copy(f32[512,128]{1,0:T(8,128)} %shard_map.91) | data formatting | bytes 524288

commit v3 on v2

--- a/solution.py
+++ b/solution.py
@@ -13,6 +13,7 @@
 F32, BF16 = jnp.float32, jnp.bfloat16
 RINGS = (16, 4)
 CTX = RINGS[0] * RINGS[1]
+SHARE = 8
 LANES = 128
 OWN = 8
 LIFT = 2.0**7.5
@@ -52,32 +53,14 @@
     lax.fori_loop(0, CTX - 1, one, 0)
 
 
-def send_blocks(*exchanges):
-    me = lax.axis_index("ctx")
-
-    def visit(peer):
-        for source, target, sent, landed in exchanges:
-            pltpu.make_async_remote_copy(
-                src_ref=source.at[peer],
-                dst_ref=target.at[me],
-                send_sem=sent,
-                recv_sem=landed,
-                device_id={"ctx": peer},
-                device_id_type=MESH,
-            ).start()
-
-    each_peer(visit)
-    for source, target, _, landed in exchanges:
-        pltpu.make_async_copy(source.at[me], target.at[me], landed).start()
-
-
-def wait_landed(target, landed):
-    pltpu.make_async_copy(target, target, landed).wait()
-
-
-def wait_sent(source, sent):
-    part = source.at[pl.ds(0, CTX - 1)]
-    pltpu.make_async_copy(part, part, sent).wait()
+def remote(source, target, sent, landed, **where):
+    return pltpu.make_async_remote_copy(
+        src_ref=source, dst_ref=target, send_sem=sent, recv_sem=landed, device_id=where, device_id_type=MESH
+    )
+
+
+def wait_bytes(ref, semaphore):
+    pltpu.make_async_copy(ref, ref, semaphore).wait()
 
 
 def split(value):
@@ -113,18 +96,24 @@
     return lax.broadcasted_iota(jnp.int32, shape, len(shape) - 1)
 
 
+GATE, EDGE, FILT, CONV, PEAK, TAIL, SIDE, SLOTS = 0, 1, 2, 3, 4, 5, 6, 6 + SHARE
+
+
 def kernel(
     feat_hbm, short_hbm, filt_hbm, skip_hbm, fwd_across_hbm, fwd_inner_hbm, inv_inner_hbm, inv_across_hbm, turn_hbm,
     out_ref,
     feat, short_flat, filt, skip, fwd_across, fwd_inner, inv_inner, inv_across, turn,
-    short, edge_rows, edge_wide, plane, plane_h,
+    short, edge_rows, edge_wide, plane, plane_h, query_part,
     gate_src, edge_src, filt_src, gate_dst, edge_dst, filt_dst,
     conv_src, peak_src, conv_dst, peak_dst, query_tail,
-    load_sem, sent, landed,
+    load_sem, sent, landed, direct,
 ):
-    me = lax.axis_index("ctx")
+    me, part_at = lax.axis_index("ctx"), lax.axis_index("dp")
+    group = (part_at - me) % SHARE
     barrier = pltpu.get_barrier_semaphore()
     each_peer(lambda peer: pl.semaphore_signal(barrier, inc=1, device_id={"ctx": peer}, device_id_type=MESH))
+    for step in range(1, SHARE):
+        pl.semaphore_signal(barrier, inc=1, device_id={"dp": (part_at + step) % SHARE}, device_id_type=MESH)
 
     pairs = (
         (feat_hbm, feat), (short_hbm, short_flat), (filt_hbm, filt), (skip_hbm, skip), (fwd_across_hbm, fwd_across),
@@ -158,6 +147,8 @@
     for i in range(count // chunk):
         row = i * chunk
         zero = jnp.zeros((chunk, LANES), F32)
+        query, query_beyond = local_feature(row)
+        query_part[pl.ds(row, chunk), :] = query
         key, key_beyond = local_feature(count + row)
         value, value_beyond = local_feature(2 * count + row)
         gated = key * value
@@ -170,6 +161,7 @@
             + pltpu.roll(jnp.where(lane < 2, value, zero), 2, axis=1)
             + pltpu.roll(key_beyond, 4, axis=1)
             + pltpu.roll(value_beyond, 6, axis=1)
+            + pltpu.roll(query_beyond, 10, axis=1)
         )
         edge = jnp.where(lane == 8, gated_peak, jnp.where(lane == 9, taps_peak, edge))
         edge_rows[pl.ds(row, chunk), :] = edge
@@ -184,33 +176,61 @@
     for q in range(CTX):
         edge_src[q] = edge_wide[q : q + 1, :]
 
-    pl.semaphore_wait(barrier, CTX - 1)
-    send_blocks((gate_src, gate_dst, sent.at[0], landed.at[0]), (edge_src, edge_dst, sent.at[1], landed.at[1]))
-    send_blocks((filt_src, filt_dst, sent.at[2], landed.at[2]))
-    tail_copy = pltpu.make_async_remote_copy(
-        src_ref=feat.at[pl.ds(0, count)],
-        dst_ref=query_tail,
-        send_sem=sent.at[5],
-        recv_sem=landed.at[5],
-        device_id={"ctx": (me + 1) % CTX},
-        device_id_type=MESH,
-    )
-    tail_copy.start()
+    pl.semaphore_wait(barrier, CTX - 1 + SHARE - 1)
+
+    filt_home = filt_dst.at[me % SHARE, me // SHARE]
+
+    def send_filter(index, carry):
+        peer = index * SHARE + group
+
+        @pl.when(peer != me)
+        def _():
+            remote(filt_src.at[peer], filt_home, sent.at[FILT], direct.at[me // SHARE], ctx=peer).start()
+
+        @pl.when(peer == me)
+        def _():
+            pltpu.make_async_copy(filt_src.at[me], filt_home, direct.at[me // SHARE]).start()
+
+        return carry
+
+    lax.fori_loop(0, CTX // SHARE, send_filter, 0)
+
+    def send_gated(peer):
+        remote(gate_src.at[peer], gate_dst.at[me], sent.at[GATE], landed.at[GATE], ctx=peer).start()
+        remote(edge_src.at[peer], edge_dst.at[me], sent.at[EDGE], landed.at[EDGE], ctx=peer).start()
+
+    each_peer(send_gated)
+    pltpu.make_async_copy(gate_src.at[me], gate_dst.at[me], landed.at[GATE]).start()
+    pltpu.make_async_copy(edge_src.at[me], edge_dst.at[me], landed.at[EDGE]).start()
+    tail = remote(edge_src, query_tail, sent.at[TAIL], landed.at[TAIL], ctx=(me + 1) % CTX)
+    tail.start()
+
+    def pass_on(index, carry):
+        slot = (me // SHARE + farthest_first(CTX // SHARE - 1 - index, CTX // SHARE)) % (CTX // SHARE)
+        block = filt_dst.at[group, slot]
+        wait_bytes(block, direct.at[slot])
+        for step in range(1, SHARE):
+            peer = (part_at + step) % SHARE
+            remote(block, block, sent.at[SIDE], landed.at[SIDE + step], dp=peer).start()
+        return carry
+
+    lax.fori_loop(0, CTX // SHARE, pass_on, 0)
+    share = filt_dst.at[group]
 
     turn_re, turn_im = turn[:CTX], turn[CTX:]
-    wait_landed(gate_dst, landed.at[0])
-    wait_landed(edge_dst, landed.at[1])
-    for p in range(CTX):
-        edge_wide[p : p + 1, :] = edge_dst[p]
+    lane = lane_of((CTX, LANES))
+    row_of = lax.broadcasted_iota(jnp.int32, (CTX, LANES), 0)
+    wait_bytes(gate_dst, landed.at[GATE])
     for i in range(8):
         part = decoded(gate_dst[pl.ds(i * 8, 8)].astype(F32))
         plane[pl.ds(i * chunk, chunk), :] = part.reshape(chunk, LANES)
+    wait_bytes(edge_dst, landed.at[EDGE])
+    for p in range(CTX):
+        edge_wide[p : p + 1, :] = edge_dst[p]
     edge = edge_wide[...]
-    row_of = lax.broadcasted_iota(jnp.int32, (CTX, LANES), 0)
     before = jnp.where(row_of >= 1, pltpu.roll(edge, 1, axis=0), 0.0)
     whole = edge + pltpu.roll(before, LANES - 4, axis=1)
     first = whole * pltpu.roll(whole, LANES - 2, axis=1)
-    lane = lane_of((CTX, LANES))
     blocks = []
     for c in range(OWN):
         at = SLOT * c
@@ -219,10 +239,12 @@
         blocks.append(jnp.where(lane == 1, first[:, at + 1 : at + 2], block))
     seen = spectrum(blocks, fwd_across[...], fwd_inner[...], turn_re, turn_im)
 
-    wait_landed(filt_dst, landed.at[2])
-    for i in range(8):
-        part = decoded(filt_dst[pl.ds(i * 8, 8)].astype(F32))
-        plane_h[pl.ds(i * chunk, chunk), :] = part.reshape(chunk, LANES)
+    for step in range(1, SHARE):
+        wait_bytes(filt_dst.at[(group - step) % SHARE], landed.at[SIDE + step])
+    for part in range(SHARE):
+        value = decoded(filt_dst[part].astype(F32))
+        for k in range(CTX // SHARE):
+            plane_h[pl.ds((k * SHARE + part) * OWN, OWN), :] = value[k]
     taps = [plane_h[pl.ds(c, CTX, stride=OWN), :] * edge[:, SLOT * c + 9 : SLOT * c + 10] for c in range(OWN)]
     response = spectrum(taps, fwd_across[...], fwd_inner[...], turn_re, turn_im)
     s_re, s_im = seen[:, :LANES], seen[:, LANES:]
@@ -242,35 +264,55 @@
     for i in range(8):
         conv_src[pl.ds(i * 8, 8)] = plane[pl.ds(i * chunk, chunk), :].reshape(8, OWN, LANES).astype(BF16)
 
-    send_blocks((conv_src, conv_dst, sent.at[3], landed.at[3]), (peak_src, peak_dst, sent.at[4], landed.at[4]))
-
-    tail_copy.wait_recv()
-    lane = lane_of((chunk, LANES))
+    def send_result(peer):
+        remote(conv_src.at[peer], conv_dst.at[me], sent.at[CONV], landed.at[CONV], ctx=peer).start()
+        remote(peak_src.at[peer], peak_dst.at[me], sent.at[PEAK], landed.at[PEAK], ctx=peer).start()
+
+    each_peer(send_result)
+    pltpu.make_async_copy(conv_src.at[me], conv_dst.at[me], landed.at[CONV]).start()
+    pltpu.make_async_copy(peak_src.at[me], peak_dst.at[me], landed.at[PEAK]).start()
+
+    tail.wait_recv()
+    shape = (8, OWN, LANES)
+    lane = lane_of(shape)
+    row_of = lax.broadcasted_iota(jnp.int32, shape, 1)
     keep = jnp.where(me > 0, 1.0, 0.0)
     for i in range(count // chunk):
         rows = pl.ds(i * chunk, chunk)
-        value, tail = feat[rows, :].astype(F32), query_tail[rows, :].astype(F32) * keep
-        taps = short[rows, :]
-        query = taps[:, 0:1] * value
-        for step in (1, 2):
-            moved = jnp.where(lane < step, pltpu.roll(tail, step, axis=1), pltpu.roll(value, step, axis=1))
-            query = query + taps[:, step : step + 1] * moved
-        plane_h[rows, :] = query
-
-    wait_landed(conv_dst, landed.at[3])
-    wait_landed(peak_dst, landed.at[4])
-    shape = (8, OWN, LANES)
-    mine = lane_of(shape) == lax.broadcasted_iota(jnp.int32, shape, 1)
+        behind = jnp.broadcast_to(query_tail[pl.ds(i * 8, 8)], shape) * keep
+        added = jnp.zeros(shape, F32)
+        for at in range(2):
+            spill = jnp.sum(jnp.where(lane == row_of * SLOT + 10 + at, behind, 0.0), axis=2, keepdims=True)
+            added = added + jnp.where(lane == at, spill, 0.0)
+        query_part[rows, :] = query_part[rows, :] + added.reshape(chunk, LANES)
+
+    wait_bytes(conv_dst, landed.at[CONV])
+    wait_bytes(peak_dst, landed.at[PEAK])
+    mine = lane == row_of
     for i in range(8):
         rows = pl.ds(i * chunk, chunk)
         peak = jnp.broadcast_to(peak_dst[pl.ds(i * 8, 8)], shape)
         peak = jnp.sum(jnp.where(mine, peak, 0.0), axis=2, keepdims=True)
         part = decoded(conv_dst[pl.ds(i * 8, 8)].astype(F32)) * peak
-        out_ref[rows, :] = plane_h[rows, :] * part.reshape(chunk, LANES)
-
-    for slot, source in enumerate((gate_src, edge_src, filt_src, conv_src, peak_src)):
-        wait_sent(source, sent.at[slot])
-    tail_copy.wait_send()
+        out_ref[rows, :] = query_part[rows, :] * part.reshape(chunk, LANES)
+
+    others = pl.ds(0, CTX - 1)
+    for slot, source in ((GATE, gate_src), (EDGE, edge_src), (CONV, conv_src), (PEAK, peak_src)):
+        wait_bytes(source.at[others], sent.at[slot])
+
+    own_group = (2 * me - part_at) % SHARE == 0
+
+    @pl.when(own_group)
+    def _():
+        wait_bytes(filt_src.at[pl.ds(0, CTX // SHARE - 1)], sent.at[FILT])
+
+    @pl.when(jnp.logical_not(own_group))
+    def _():
+        wait_bytes(filt_src.at[pl.ds(0, CTX // SHARE)], sent.at[FILT])
+
+    for _ in range(1, SHARE):
+        wait_bytes(share, sent.at[SIDE])
+    tail.wait_send()
 
 
 def halves(table):
@@ -314,15 +356,18 @@
             pltpu.VMEM((CTX, LANES), F32),
             pltpu.VMEM((count, LANES), F32),
             pltpu.VMEM((count, LANES), F32),
+            pltpu.VMEM((count, LANES), F32),
             pltpu.VMEM(rows, BF16), pltpu.VMEM(row, F32), pltpu.VMEM(rows, BF16),
-            pltpu.VMEM(rows, BF16), pltpu.VMEM(row, F32), pltpu.VMEM(rows, BF16),
+            pltpu.VMEM(rows, BF16), pltpu.VMEM(row, F32), pltpu.VMEM((SHARE, CTX // SHARE, OWN, LANES), BF16),
             pltpu.VMEM(rows, BF16), pltpu.VMEM(row, F32),
             pltpu.VMEM(rows, BF16), pltpu.VMEM(row, F32),
-            pltpu.VMEM((count, LANES), BF16),
+            pltpu.VMEM(row, F32),
             pltpu.SemaphoreType.DMA((len(operands),)),
-            pltpu.SemaphoreType.DMA((6,)),
-            pltpu.SemaphoreType.DMA((6,)),
+            pltpu.SemaphoreType.DMA((SLOTS,)),
+            pltpu.SemaphoreType.DMA((SLOTS,)),
+            pltpu.SemaphoreType.DMA((CTX // SHARE,)),
         ]
+        operands = [pltpu.with_memory_space_constraint(value, pltpu.HBM) for value in operands]
         return pl.pallas_call(
             kernel,
             out_shape=jax.ShapeDtypeStruct((count, LANES), F32),
@@ -330,7 +375,7 @@
             out_specs=pl.BlockSpec(memory_space=pltpu.VMEM),
             scratch_shapes=scratch,
             compiler_params=pltpu.CompilerParams(
-                collective_id=0, has_side_effects=True, vmem_limit_bytes=60 * 1024 * 1024
+                collective_id=0, has_side_effects=True, vmem_limit_bytes=48 * 1024 * 1024
             ),
         )(*operands)
 

time: 46.9 us -> 45.2 us (0.964)
  the two profiles are of different devices: /device:TPU:24 before, /device:TPU:1 now
where the time goes in v3:
time: 45.2 us; the launch traced here: 45.1 us
  Pallas kernels  44.4 us (98%)
  local copies, waits for them, and re-layouts  0.71 us (2%)
    pallas_call x1, Pallas kernels, body(): pl.pallas_call(kernel, out_shape=jax.ShapeDtypeStruct((count, LANES), F32...  44.4 us

profile of v3, /device:TPU:1, one launch (start us, length us, event | category | flops | bytes accessed | tf_op | source)
XLA Modules:
  0.0 45.1 jit_solution(12444054878235986779)
XLA Ops:
  0.0 44.4 %shard_map.91 = f32[512,128]{1,0:T(8,128)S(1)} custom-call(bf16[1536,128]{1,0:T(8,128)(2,1)} %feat_hbm.1, f32[3,1536]{1,0:T(4,128)} %bitcast.1, f32[512,128]{1,0:T(8,128)} %filt_hbm.1, f32[512]{0:T(512)} %skip_hbm.1, bf16[128,256]{1,0:T(8,128)(2,1)} %constant.10.clone.fwd_across_hbm, bf16[768,256]{1,0:T(8,128)(2,1)} %constant.11.clone.fwd_inner_hbm, ...), custom_call_target="tpu_custom_call" | custom-call | tf_op jit(solution)/shard_map/pallas_call | solution.py:371
  44.4 0.7 %copy.11 = f32[512,128]{1,0:T(8,128)} copy(f32[512,128]{1,0:T(8,128)S(1)} %shard_map.91) | data formatting | bytes 524288

commit v4 on v3

--- a/solution.py
+++ b/solution.py
@@ -36,21 +36,29 @@
 
 
 def farthest_first(index, extent):
-    half, step = extent // 2, (index + 1) // 2
-    return half + step * (1 - 2 * (index % 2))
-
-
-def each_peer(visit):
+    step = (index + 1) // 2
+    return jnp.where(lax.rem(index, 2) == 0, extent // 2 + step, extent // 2 - step)
+
+
+def each_peer(visit, begin=0):
     me = lax.axis_index("ctx")
-    at_z, at_x = me // RINGS[1], me % RINGS[1]
-
-    def one(index, carry):
-        to_z = (at_z + farthest_first(index // RINGS[1], RINGS[0])) % RINGS[0]
-        to_x = (at_x + farthest_first(index % RINGS[1], RINGS[1])) % RINGS[1]
-        visit(to_z * RINGS[1] + to_x)
+    at_z, at_x = lax.div(me, RINGS[1]), lax.rem(me, RINGS[1])
+    to_x = [lax.rem(at_x + step, RINGS[1]) for step in (2, 1, 3)]
+
+    def plane(index, carry):
+        step = lax.rem(index + begin, RINGS[0])
+        step = lax.rem(at_z + farthest_first(step, RINGS[0]), RINGS[0])
+        row = step * RINGS[1]
+        for x in to_x:
+            visit(row + x)
+
+        @pl.when(step != at_z)
+        def _():
+            visit(row + at_x)
+
         return carry
 
-    lax.fori_loop(0, CTX - 1, one, 0)
+    lax.fori_loop(0, RINGS[0], plane, 0)
 
 
 def remote(source, target, sent, landed, **where):
@@ -109,11 +117,13 @@
     load_sem, sent, landed, direct,
 ):
     me, part_at = lax.axis_index("ctx"), lax.axis_index("dp")
-    group = (part_at - me) % SHARE
+    member = lax.rem(part_at, SHARE)
+    group = lax.rem(member - lax.rem(me, SHARE) + SHARE, SHARE)
+    others = [part_at - member + lax.rem(member + step, SHARE) for step in range(1, SHARE)]
     barrier = pltpu.get_barrier_semaphore()
     each_peer(lambda peer: pl.semaphore_signal(barrier, inc=1, device_id={"ctx": peer}, device_id_type=MESH))
-    for step in range(1, SHARE):
-        pl.semaphore_signal(barrier, inc=1, device_id={"dp": (part_at + step) % SHARE}, device_id_type=MESH)
+    for peer in others:
+        pl.semaphore_signal(barrier, inc=1, device_id={"dp": peer}, device_id_type=MESH)
 
     pairs = (
         (feat_hbm, feat), (short_hbm, short_flat), (filt_hbm, filt), (skip_hbm, skip), (fwd_across_hbm, fwd_across),
@@ -181,7 +191,8 @@
     filt_home = filt_dst.at[me % SHARE, me // SHARE]
 
     def send_filter(index, carry):
-        peer = index * SHARE + group
+        place = lax.rem(me // SHARE + farthest_first(index, CTX // SHARE), CTX // SHARE)
+        peer = place * SHARE + group
 
         @pl.when(peer != me)
         def _():
@@ -199,19 +210,20 @@
         remote(gate_src.at[peer], gate_dst.at[me], sent.at[GATE], landed.at[GATE], ctx=peer).start()
         remote(edge_src.at[peer], edge_dst.at[me], sent.at[EDGE], landed.at[EDGE], ctx=peer).start()
 
-    each_peer(send_gated)
+    each_peer(send_gated, jnp.where(me < 4 * RINGS[1], 0, 7))
     pltpu.make_async_copy(gate_src.at[me], gate_dst.at[me], landed.at[GATE]).start()
     pltpu.make_async_copy(edge_src.at[me], edge_dst.at[me], landed.at[EDGE]).start()
     tail = remote(edge_src, query_tail, sent.at[TAIL], landed.at[TAIL], ctx=(me + 1) % CTX)
     tail.start()
 
+    my_slot = me // SHARE
+
     def pass_on(index, carry):
-        slot = (me // SHARE + farthest_first(CTX // SHARE - 1 - index, CTX // SHARE)) % (CTX // SHARE)
+        slot = lax.rem(my_slot + farthest_first(CTX // SHARE - 1 - index, CTX // SHARE), CTX // SHARE)
         block = filt_dst.at[group, slot]
         wait_bytes(block, direct.at[slot])
-        for step in range(1, SHARE):
-            peer = (part_at + step) % SHARE
-            remote(block, block, sent.at[SIDE], landed.at[SIDE + step], dp=peer).start()
+        for step, peer in enumerate(others):
+            remote(block, block, sent.at[SIDE], landed.at[SIDE + 1 + step], dp=peer).start()
         return carry
 
     lax.fori_loop(0, CTX // SHARE, pass_on, 0)
@@ -296,11 +308,11 @@
         part = decoded(conv_dst[pl.ds(i * 8, 8)].astype(F32)) * peak
         out_ref[rows, :] = query_part[rows, :] * part.reshape(chunk, LANES)
 
-    others = pl.ds(0, CTX - 1)
+    away = pl.ds(0, CTX - 1)
     for slot, source in ((GATE, gate_src), (EDGE, edge_src), (CONV, conv_src), (PEAK, peak_src)):
-        wait_bytes(source.at[others], sent.at[slot])
-
-    own_group = (2 * me - part_at) % SHARE == 0
+        wait_bytes(source.at[away], sent.at[slot])
+
+    own_group = group == lax.rem(me, SHARE)
 
     @pl.when(own_group)
     def _():

time: 45.2 us -> 43.1 us (0.954)
  the two profiles are of different devices: /device:TPU:1 before, /device:TPU:24 now
where the time goes in v4:
time: 43.1 us; the launch traced here: 42.5 us
  Pallas kernels  41.8 us (97%)
  local copies, waits for them, and re-layouts  0.71 us (2%)
    pallas_call x1, Pallas kernels, body(): pl.pallas_call(kernel, out_shape=jax.ShapeDtypeStruct((count, LANES), F32...  41.8 us

profile of v4, /device:TPU:24, one launch (start us, length us, event | category | flops | bytes accessed | tf_op | source)
XLA Modules:
  0.0 42.5 jit_solution(16011606345842681392)
XLA Ops:
  0.0 41.8 %shard_map.91 = f32[512,128]{1,0:T(8,128)S(1)} custom-call(bf16[1536,128]{1,0:T(8,128)(2,1)} %feat_hbm.1, f32[3,1536]{1,0:T(4,128)} %bitcast.1, f32[512,128]{1,0:T(8,128)} %filt_hbm.1, f32[512]{0:T(512)} %skip_hbm.1, bf16[128,256]{1,0:T(8,128)(2,1)} %constant.10.clone.fwd_across_hbm, bf16[768,256]{1,0:T(8,128)(2,1)} %constant.11.clone.fwd_inner_hbm, ...), custom_call_target="tpu_custom_call" | custom-call | tf_op jit(solution)/shard_map/pallas_call | solution.py:383
  41.8 0.7 %copy.11 = f32[512,128]{1,0:T(8,128)} copy(f32[512,128]{1,0:T(8,128)S(1)} %shard_map.91) | data formatting | bytes 524288

commit v5 on v4

--- a/solution.py
+++ b/solution.py
@@ -13,7 +13,7 @@
 F32, BF16 = jnp.float32, jnp.bfloat16
 RINGS = (16, 4)
 CTX = RINGS[0] * RINGS[1]
-SHARE = 8
+SHARE = 4
 LANES = 128
 OWN = 8
 LIFT = 2.0**7.5
@@ -210,7 +210,7 @@
         remote(gate_src.at[peer], gate_dst.at[me], sent.at[GATE], landed.at[GATE], ctx=peer).start()
         remote(edge_src.at[peer], edge_dst.at[me], sent.at[EDGE], landed.at[EDGE], ctx=peer).start()
 
-    each_peer(send_gated, jnp.where(me < 4 * RINGS[1], 0, 7))
+    each_peer(send_gated, jnp.where(me < 2 * RINGS[1], 0, 7))
     pltpu.make_async_copy(gate_src.at[me], gate_dst.at[me], landed.at[GATE]).start()
     pltpu.make_async_copy(edge_src.at[me], edge_dst.at[me], landed.at[EDGE]).start()
     tail = remote(edge_src, query_tail, sent.at[TAIL], landed.at[TAIL], ctx=(me + 1) % CTX)

time: 43.1 us -> 42.6 us (0.988)
  no operation moved by 1% of the time
where the time goes in v5:
time: 42.6 us; the launch traced here: 42.5 us
  Pallas kernels  41.7 us (98%)
  local copies, waits for them, and re-layouts  0.71 us (2%)
    pallas_call x1, Pallas kernels, body(): pl.pallas_call(kernel, out_shape=jax.ShapeDtypeStruct((count, LANES), F32...  41.7 us

profile of v5, /device:TPU:24, one launch (start us, length us, event | category | flops | bytes accessed | tf_op | source)
XLA Modules:
  0.0 42.5 jit_solution(5026327644379028015)
XLA Ops:
  0.0 41.7 %shard_map.91 = f32[512,128]{1,0:T(8,128)S(1)} custom-call(bf16[1536,128]{1,0:T(8,128)(2,1)} %feat_hbm.1, f32[3,1536]{1,0:T(4,128)} %bitcast.1, f32[512,128]{1,0:T(8,128)} %filt_hbm.1, f32[512]{0:T(512)} %skip_hbm.1, bf16[128,256]{1,0:T(8,128)(2,1)} %constant.10.clone.fwd_across_hbm, bf16[768,256]{1,0:T(8,128)(2,1)} %constant.11.clone.fwd_inner_hbm, ...), custom_call_target="tpu_custom_call" | custom-call | tf_op jit(solution)/shard_map/pallas_call | solution.py:383
  41.7 0.7 %copy.11 = f32[512,128]{1,0:T(8,128)} copy(f32[512,128]{1,0:T(8,128)S(1)} %shard_map.91) | data formatting | bytes 524288

commit v6 on v5

--- a/solution.py
+++ b/solution.py
@@ -251,12 +251,16 @@
         blocks.append(jnp.where(lane == 1, first[:, at + 1 : at + 2], block))
     seen = spectrum(blocks, fwd_across[...], fwd_inner[...], turn_re, turn_im)
 
-    for step in range(1, SHARE):
-        wait_bytes(filt_dst.at[(group - step) % SHARE], landed.at[SIDE + step])
-    for part in range(SHARE):
+    def unpack_filter(part):
         value = decoded(filt_dst[part].astype(F32))
         for k in range(CTX // SHARE):
-            plane_h[pl.ds((k * SHARE + part) * OWN, OWN), :] = value[k]
+            plane_h[pl.ds(pl.multiple_of((k * SHARE + part) * OWN, OWN), OWN), :] = value[k]
+
+    unpack_filter(group)
+    for step in range(1, SHARE):
+        part = lax.rem(group - step + SHARE, SHARE)
+        wait_bytes(filt_dst.at[part], landed.at[SIDE + step])
+        unpack_filter(part)
     taps = [plane_h[pl.ds(c, CTX, stride=OWN), :] * edge[:, SLOT * c + 9 : SLOT * c + 10] for c in range(OWN)]
     response = spectrum(taps, fwd_across[...], fwd_inner[...], turn_re, turn_im)
     s_re, s_im = seen[:, :LANES], seen[:, LANES:]

time: 42.6 us -> 42.6 us (level)
  no operation moved by 1% of the time
where the time goes in v6:
time: 42.6 us; the launch traced here: 42.5 us
  Pallas kernels  41.8 us (98%)
  local copies, waits for them, and re-layouts  0.71 us (2%)
    pallas_call x1, Pallas kernels, body(): pl.pallas_call(kernel, out_shape=jax.ShapeDtypeStruct((count, LANES), F32...  41.8 us

profile of v6, /device:TPU:24, one launch (start us, length us, event | category | flops | bytes accessed | tf_op | source)
XLA Modules:
  0.0 42.5 jit_solution(1703682753082315607)
XLA Ops:
  0.0 41.8 %shard_map.91 = f32[512,128]{1,0:T(8,128)S(1)} custom-call(bf16[1536,128]{1,0:T(8,128)(2,1)} %feat_hbm.1, f32[3,1536]{1,0:T(4,128)} %bitcast.1, f32[512,128]{1,0:T(8,128)} %filt_hbm.1, f32[512]{0:T(512)} %skip_hbm.1, bf16[128,256]{1,0:T(8,128)(2,1)} %constant.10.clone.fwd_across_hbm, bf16[768,256]{1,0:T(8,128)(2,1)} %constant.11.clone.fwd_inner_hbm, ...), custom_call_target="tpu_custom_call" | custom-call | tf_op jit(solution)/shard_map/pallas_call | solution.py:387
  41.8 0.7 %copy.11 = f32[512,128]{1,0:T(8,128)} copy(f32[512,128]{1,0:T(8,128)S(1)} %shard_map.91) | data formatting | bytes 524288

commit v7 on v6

--- a/solution.py
+++ b/solution.py
@@ -97,7 +97,8 @@
         re, im = part[:, :LANES], part[:, LANES:]
         columns.append(jnp.concatenate([re * turn_re + im * turn_im, im * turn_re - re * turn_im], axis=0))
     high, low = split(jnp.concatenate(columns, axis=1))
-    return jnp.dot(across, jnp.concatenate([high, low, high], axis=0), preferred_element_type=F32)
+    sums = jnp.dot(across, jnp.concatenate([high, low], axis=0), preferred_element_type=F32)
+    return sums[:CTX] + sums[CTX:]
 
 
 def lane_of(shape):
@@ -343,7 +344,7 @@
     high, low = halves(np.concatenate([np.cos(outer), -np.sin(outer)], axis=0))
     fwd_across = np.concatenate([high, high, low, low], axis=1)
     high, low = halves(np.concatenate([np.cos(outer.T), -np.sin(outer.T)], axis=1) * (2.0 / points))
-    inv_across = np.concatenate([high, high, low], axis=1)
+    inv_across = np.block([[high, high], [low, np.zeros_like(low)]])
     inner = 2 * math.pi / LANES * (np.outer(s, k2) % LANES)
     cos, sin = np.cos(inner), np.sin(inner)
     high, low = halves(np.block([[cos, -sin], [sin, cos]]))

time: 42.6 us -> 42.5 us (level)
  no operation moved by 1% of the time
where the time goes in v7:
time: 42.5 us; the launch traced here: 42.4 us
  Pallas kernels  41.7 us (98%)
  local copies, waits for them, and re-layouts  0.71 us (2%)
    pallas_call x1, Pallas kernels, body(): pl.pallas_call(kernel, out_shape=jax.ShapeDtypeStruct((count, LANES), F32...  41.7 us

profile of v7, /device:TPU:24, one launch (start us, length us, event | category | flops | bytes accessed | tf_op | source)
XLA Modules:
  0.0 42.4 jit_solution(17504295582351985562)
XLA Ops:
  0.0 41.7 %shard_map.91 = f32[512,128]{1,0:T(8,128)S(1)} custom-call(bf16[1536,128]{1,0:T(8,128)(2,1)} %feat_hbm.1, f32[3,1536]{1,0:T(4,128)} %bitcast.1, f32[512,128]{1,0:T(8,128)} %filt_hbm.1, f32[512]{0:T(512)} %skip_hbm.1, bf16[128,256]{1,0:T(8,128)(2,1)} %constant.10.clone.fwd_across_hbm, bf16[768,256]{1,0:T(8,128)(2,1)} %constant.11.clone.fwd_inner_hbm, ...), custom_call_target="tpu_custom_call" | custom-call | tf_op jit(solution)/shard_map/pallas_call | solution.py:388
  41.7 0.7 %copy.11 = f32[512,128]{1,0:T(8,128)} copy(f32[512,128]{1,0:T(8,128)S(1)} %shard_map.91) | data formatting | bytes 524288
